TPU v7x, 128 devices: a whole 4x4x4 slice. The times are simulated.
128 devices in a mesh: rows: 32 (over z, y, core), vecs: 4 (over x).
Axes of the slice: x: 4, y: 4, z: 4, core: 2. Of those that a mesh axis runs over, the one named last changes fastest.
Arguments:
- vectors: bfloat16 [131072, 1024], P('rows', 'vecs'), may hold values from -6 to 6, as said below
- blocks: bfloat16 [1024, 5, 128, 128], P('rows'), may hold values from -0.25 to 0.25
- columns: int32 [1024, 5], P('rows'), may hold values from 0 to 1023, as said below
Outputs:
- basis: float32 [131072, 1024], P('rows', 'vecs')
Inputs may be any that keep to these rules, and one draw needn't show every extreme that they name: Each block row i names 5 block columns of the form i + d clipped to 0 .. 1023, with distinct d in -8 .. 8; near the grid's ends some may repeat. `vectors`: entries of order one.
All inputs are finite; a program needn't handle non-finite values.
Results may differ from a plain program's by a relative error of at most 0.0075.
Values may be sent and summed in bfloat16 or wider, within the bound.
No kernel may reach another device: no remote copies, remote signals or barrier semaphores. Data moves between devices by JAX's collectives and lax.ppermute only.
A program may use at most 128 MiB of HBM per device.

v0:
```python
import jax
import jax.numpy as jnp
from jax import lax
from jax.sharding import PartitionSpec as P

DEGREE = 4
filter_center = 0.25
filter_radius = 1.25


def with_halo(shard, sides, width):
    for axis, dim in sides:
        count, length = (lax.axis_size(axis), shard.shape[dim])
        up = [(i, (i + 1) % count) for i in range(count - 1)]
        down = [(j, i) for i, j in up]
        last = lax.slice_in_dim(shard, length - width, length, axis=dim)
        first = lax.slice_in_dim(shard, 0, width, axis=dim)
        before = lax.ppermute(last, axis, up)
        after = lax.ppermute(first, axis, down)
        shard = jnp.concatenate([before, shard, after], axis=dim)
    return shard


def product(vec_bf, blocks, local_index):
    block_rows = blocks.shape[0]
    size_b = blocks.shape[2]
    width = vec_bf.shape[1]
    reach = block_rows // 4
    padded = with_halo(vec_bf, (("rows", 0),), reach * size_b)
    stacked = padded.reshape(block_rows + 2 * reach, size_b, width)
    picked = stacked[local_index]
    result = jnp.einsum("rjab,rjbk->rak", blocks, picked, preferred_element_type=jnp.float32)
    return result.reshape(block_rows * size_b, width)


def split_apply(left_bf, factor):
    factor_high = factor.astype(jnp.bfloat16)
    factor_low = (factor - factor_high.astype(jnp.float32)).astype(jnp.bfloat16)
    first = jnp.dot(left_bf, factor_high.T, preferred_element_type=jnp.float32)
    second = jnp.dot(left_bf, factor_low.T, preferred_element_type=jnp.float32)
    return first + second


def shards(vectors, blocks, columns):
    block_rows = blocks.shape[0]
    reach = block_rows // 4
    first_row = lax.axis_index("rows") * block_rows
    local_index = columns - first_row + reach
    total_rows = vectors.shape[0] * lax.axis_size("rows")
    older = vectors.astype(jnp.float32)
    current = (product(vectors, blocks, local_index) - filter_center * older) / filter_radius
    for iteration in range(1, DEGREE):
        rounded = current.astype(jnp.bfloat16)
        newer = (
            2.0 * (product(rounded, blocks, local_index) - filter_center * current) / filter_radius
            - older
        )
        older = current
        current = newer
    final = current.astype(jnp.bfloat16)
    panel_width = final.shape[1]
    full_width = panel_width * lax.axis_size("vecs")
    identity = jnp.eye(full_width, dtype=jnp.float32)
    whole_block = lax.all_gather(final, "vecs", axis=1, tiled=True)
    panel = jnp.dot(final.T, whole_block, preferred_element_type=jnp.float32)
    summed = lax.psum(panel, "rows")
    gram_matrix = lax.all_gather(summed, "vecs", axis=0, tiled=True) / total_rows
    lower = jnp.linalg.cholesky(gram_matrix)
    inverse = lax.linalg.triangular_solve(lower, identity, left_side=True, lower=True)
    own_rows = lax.dynamic_slice_in_dim(
        inverse, lax.axis_index("vecs") * panel_width, panel_width, 0
    )
    return split_apply(whole_block, own_rows)


def solution(mesh):
    in_specs = (P("rows", "vecs"), P("rows", None, None, None), P("rows", None))
    out_specs = P("rows", "vecs")
    return jax.shard_map(shards, mesh=mesh, in_specs=in_specs, out_specs=out_specs, check_vma=False)
```

profile of v0, /device:TPU:1, one launch (start us, length us, event | category | flops | bytes accessed | tf_op | source)
XLA Modules:
  0.0 772.8 jit_solution(1005979501189157616)
XLA Ops:
  25.1 7.6 gather_fusion
  32.7 7.5 fusion.88
  56.7 9.5 %gather_fusion.1 = bf16[160,128,256]{2,1,0:T(8,128)(2,1)} fusion(bf16[48,128,256]{2,1,0:T(8,128)(2,1)} %bitcast.194, s32[1024]{0:T(1024)S(1)} %pad_clamp_fusion), kind=kCustom, calls=%fused_computation.1 | custom fusion | bytes 20972160 | tf_op jit(solution)/shard_map/gather | solution.py:31
  66.2 7.5 fusion.89
  90.1 9.5 %gather_fusion.2 = bf16[160,128,256]{2,1,0:T(8,128)(2,1)} fusion(bf16[48,128,256]{2,1,0:T(8,128)(2,1)} %bitcast.195, s32[1024]{0:T(1024)S(1)} %pad_clamp_fusion), kind=kCustom, calls=%fused_computation.2 | custom fusion | bytes 20972160 | tf_op jit(solution)/shard_map/gather | solution.py:31
  99.6 7.5 fusion.90
  118.3 6.1 collective-permute-done.7
  126.3 9.5 %gather_fusion.3 = bf16[160,128,256]{2,1,0:T(8,128)(2,1)} fusion(bf16[48,128,256]{2,1,0:T(8,128)(2,1)} %bitcast.193, s32[1024]{0:T(1024)S(1)} %pad_clamp_fusion), kind=kCustom, calls=%fused_computation.3 | custom fusion | bytes 20972160 | tf_op jit(solution)/shard_map/gather | solution.py:31
  135.7 7.5 fusion.91
  149.4 94.6 %all-gather.3.cloned.1.call-done = bf16[4096,1024]{1,0:T(8,128)(2,1)} async-done(((bf16[4096,256]{1,0:T(8,128)(2,1)}), bf16[4096,1024]{1,0:T(8,128)(2,1)}) %all-gather.3.cloned.1.call-update) | async-done | bytes 8388624 | tf_op jit(solution)/shard_map/all_gather | solution.py:64
  244.0 8.4 %fusion.87 = f32[256,1024]{0,1:T(8,128)} fusion(bf16[4096,256]{1,0:T(8,128)(2,1)} %fusion.3, bf16[4096,1024]{1,0:T(8,128)(2,1)} %all-gather.3.cloned.1.call-done), kind=kOutput, calls=%fused_computation.195 | convolution fusion | flops 2147483648 | bytes 11534336 | tf_op jit(solution)/shard_map/dot_general | solution.py:65
  252.5 106.3 %all-reduce.3.cloned.1.call-done = f32[256,1024]{0,1:T(8,128)} async-done(((f32[256,1024]{0,1:T(8,128)}), f32[256,1024]{0,1:T(8,128)}) %all-reduce.3.cloned.1.call-update) | async-done | bytes 1048592 | tf_op jit(solution)/shard_map/psum | solution.py:66
  361.7 46.9 %all-gather.5.cloned.1.call-done = f32[1024,1024]{0,1:T(8,128)} async-done(((f32[256,1024]{0,1:T(8,128)}), f32[1024,1024]{0,1:T(8,128)}) %all-gather.5.cloned.1.call-update) | async-done | bytes 4194320 | tf_op jit(solution)/shard_map/all_gather | solution.py:67
  408.6 5.0 broadcast_multiply_fusion
  413.6 5.5 copy.8
  425.5 11.7 %cholesky.223 = f32[128,128]{1,0:T(8,128)S(1)} custom-call(f32[128,128]{1,0:T(8,128)S(1)} %cholesky.580), custom_call_target="Cholesky" | custom-call | tf_op jit(solution)/shard_map/jit(cholesky)/cholesky | solution.py:68
  437.3 9.8 %custom-call.62 = f32[1,128,128]{1,2,0:T(8,128)S(1)} custom-call(f32[1,128,128]{2,1,0:T(8,128)S(1)} %get-tuple-element.77), custom_call_target="InvertDiagBlocksLowerTriangular" | custom-call | tf_op jit(solution)/shard_map/jit(cholesky)/cholesky | solution.py:68
  453.5 11.9 %cholesky.244 = f32[128,128]{1,0:T(8,128)S(1)} custom-call(f32[128,128]{1,0:T(8,128)S(1)} %cholesky.584), custom_call_target="Cholesky" | custom-call | tf_op jit(solution)/shard_map/jit(cholesky)/cholesky | solution.py:68
  466.1 9.8 %custom-call.63 = f32[1,128,128]{1,2,0:T(8,128)S(1)} custom-call(f32[1,128,128]{2,1,0:T(8,128)S(1)} %get-tuple-element.74), custom_call_target="InvertDiagBlocksLowerTriangular" | custom-call | tf_op jit(solution)/shard_map/jit(cholesky)/cholesky | solution.py:68
  479.2 11.7 %cholesky.468 = f32[128,128]{1,0:T(8,128)S(1)} custom-call(f32[128,128]{1,0:T(8,128)S(1)} %cholesky.589), custom_call_target="Cholesky" | custom-call | tf_op jit(solution)/shard_map/jit(cholesky)/cholesky | solution.py:68
  492.2 9.8 %custom-call.64 = f32[1,128,128]{1,2,0:T(8,128)S(1)} custom-call(f32[1,128,128]{2,1,0:T(8,128)S(1)} %get-tuple-element.71), custom_call_target="InvertDiagBlocksLowerTriangular" | custom-call | tf_op jit(solution)/shard_map/jit(cholesky)/cholesky | solution.py:68
  505.5 12.1 %cholesky.487 = f32[128,128]{1,0:T(8,128)S(1)} custom-call(f32[128,128]{1,0:T(8,128)S(1)} %cholesky.594), custom_call_target="Cholesky" | custom-call | tf_op jit(solution)/shard_map/jit(cholesky)/cholesky | solution.py:68
  519.0 9.8 %custom-call.65 = f32[1,128,128]{1,2,0:T(8,128)S(1)} custom-call(f32[1,128,128]{2,1,0:T(8,128)S(1)} %get-tuple-element.68), custom_call_target="InvertDiagBlocksLowerTriangular" | custom-call | tf_op jit(solution)/shard_map/jit(cholesky)/cholesky | solution.py:68
  532.2 11.7 %cholesky.506 = f32[128,128]{1,0:T(8,128)S(1)} custom-call(f32[128,128]{1,0:T(8,128)S(1)} %cholesky.599), custom_call_target="Cholesky" | custom-call | tf_op jit(solution)/shard_map/jit(cholesky)/cholesky | solution.py:68
  545.2 10.0 %custom-call.66 = f32[1,128,128]{1,2,0:T(8,128)S(1)} custom-call(f32[1,128,128]{2,1,0:T(8,128)S(1)} %get-tuple-element.65), custom_call_target="InvertDiagBlocksLowerTriangular" | custom-call | tf_op jit(solution)/shard_map/jit(cholesky)/cholesky | solution.py:68
  558.5 11.7 %cholesky.526 = f32[128,128]{1,0:T(8,128)S(1)} custom-call(f32[128,128]{1,0:T(8,128)S(1)} %cholesky.604), custom_call_target="Cholesky" | custom-call | tf_op jit(solution)/shard_map/jit(cholesky)/cholesky | solution.py:68
  571.5 9.8 %custom-call.67 = f32[1,128,128]{1,2,0:T(8,128)S(1)} custom-call(f32[1,128,128]{2,1,0:T(8,128)S(1)} %get-tuple-element.62), custom_call_target="InvertDiagBlocksLowerTriangular" | custom-call | tf_op jit(solution)/shard_map/jit(cholesky)/cholesky | solution.py:68
  584.2 11.9 %cholesky.546 = f32[128,128]{1,0:T(8,128)S(1)} custom-call(f32[128,128]{1,0:T(8,128)S(1)} %cholesky.609), custom_call_target="Cholesky" | custom-call | tf_op jit(solution)/shard_map/jit(cholesky)/cholesky | solution.py:68
  597.5 9.8 %custom-call.68 = f32[1,128,128]{1,2,0:T(8,128)S(1)} custom-call(f32[1,128,128]{2,1,0:T(8,128)S(1)} %get-tuple-element.59), custom_call_target="InvertDiagBlocksLowerTriangular" | custom-call | tf_op jit(solution)/shard_map/jit(cholesky)/cholesky | solution.py:68
  609.9 11.7 %cholesky.564 = f32[128,128]{1,0:T(8,128)S(1)} custom-call(f32[128,128]{1,0:T(8,128)S(1)} %convolution_subtract_fusion.11), custom_call_target="Cholesky" | custom-call | tf_op jit(solution)/shard_map/jit(cholesky)/cholesky | solution.py:68
  633.4 23.9 %while.1 = (s32[]{:T(128)}, f32[1024,1024]{1,0:T(8,128)}, s32[8,2]{0,1:T(2,128)S(1)}, f32[8,128,128]{2,1,0:T(8,128)S(1)}, s32[]{:T(128)}) while((s32[]{:T(128)}, f32[1024,1024]{1,0:T(8,128)}, s32[8,2]{0,1:T(2,128)S(1)}, f32[8,128,128]{2,1,0:T(8,128)S(1)}, s32[]{:T(128)}) %tuple.61), condition=%wide.while_cond, body=%wide.while_body.sunk | while | flops 2 | bytes 131189 | solution.py:69
  657.3 79.0 %custom-call.69 = f32[8,128,128]{1,2,0:T(8,128)S(1)} custom-call(f32[8,128,128]{2,1,0:T(8,128)S(1)} %get-tuple-element.12), custom_call_target="InvertDiagBlocksLowerTriangular" | custom-call | tf_op jit(solution)/shard_map/triangular_solve | solution.py:69
  (153 shorter events, 172.5 us)
Async XLA Ops:
  6.5 237.5 %all-gather.3.cloned.1.call-start = ((), (), s32[]{:S(2)}) async-start(), calls=%async_computation | async-start | bytes 10485760 | tf_op jit(solution)/shard_map/all_gather | solution.py:64
  7.8 10.7 %collective-permute-start = (bf16[1024,256]{1,0:T(8,128)(2,1)S(1)}, bf16[1024,256]{1,0:T(8,128)(2,1)S(1)}, u32[]{:S(2)}, u32[]{:S(2)}) collective-permute-start(bf16[1024,256]{1,0:T(8,128)(2,1)S(1)} %get-tuple-element.29), channel_id=1, source_target_pairs={{0,4},{4,8},{8,12},{12,16},{16,20},{20,24},{24,28},{28,32},{32,36}... | collective-permute-start | bytes 1572872 | tf_op jit(solution)/shard_map/ppermute | solution.py:18
  12.4 10.6 %collective-permute-start.1 = (bf16[1024,256]{1,0:T(8,128)(2,1)S(1)}, bf16[1024,256]{1,0:T(8,128)(2,1)}, u32[]{:S(2)}, u32[]{:S(2)}) collective-permute-start(bf16[1024,256]{1,0:T(8,128)(2,1)S(1)} %get-tuple-element.30), channel_id=1, source_target_pairs={{4,0},{8,4},{12,8},{16,12},{20,16},{24,20},{28,24},{32,28},{36,32}... | collective-permute-start | bytes 1572872 | tf_op jit(solution)/shard_map/ppermute | solution.py:19
  18.5 0.8 copy-start.12
  32.7 7.5 copy-start.7
  40.3 2.0 copy-start
  42.4 8.0 %collective-permute-start.2 = (bf16[1024,256]{1,0:T(8,128)(2,1)S(1)}, bf16[1024,256]{1,0:T(8,128)(2,1)S(1)}, u32[]{:S(2)}, u32[]{:S(2)}) collective-permute-start(bf16[1024,256]{1,0:T(8,128)(2,1)S(1)} %get-tuple-element.27), channel_id=1, source_target_pairs={{0,4},{4,8},{8,12},{12,16},{16,20},{20,24},{24,28},{28,32},{32,36}... | collective-permute-start | bytes 1572872 | tf_op jit(solution)/shard_map/ppermute | solution.py:18
  44.3 10.5 %collective-permute-start.3 = (bf16[1024,256]{1,0:T(8,128)(2,1)S(1)}, bf16[1024,256]{1,0:T(8,128)(2,1)S(1)}, u32[]{:S(2)}, u32[]{:S(2)}) collective-permute-start(bf16[1024,256]{1,0:T(8,128)(2,1)S(1)} %get-tuple-element.28), channel_id=1, source_target_pairs={{4,0},{8,4},{12,8},{16,12},{20,16},{24,20},{28,24},{32,28},{36,32}... | collective-permute-start | bytes 1572872 | tf_op jit(solution)/shard_map/ppermute | solution.py:19
  66.2 7.5 copy-start.1
  73.7 2.1 copy-start.4
  75.9 8.0 %collective-permute-start.4 = (bf16[1024,256]{1,0:T(8,128)(2,1)S(1)}, bf16[1024,256]{1,0:T(8,128)(2,1)S(1)}, u32[]{:S(2)}, u32[]{:S(2)}) collective-permute-start(bf16[1024,256]{1,0:T(8,128)(2,1)S(1)} %get-tuple-element.25), channel_id=1, source_target_pairs={{0,4},{4,8},{8,12},{12,16},{16,20},{20,24},{24,28},{28,32},{32,36}... | collective-permute-start | bytes 1572872 | tf_op jit(solution)/shard_map/ppermute | solution.py:18
  77.8 10.5 %collective-permute-start.5 = (bf16[1024,256]{1,0:T(8,128)(2,1)S(1)}, bf16[1024,256]{1,0:T(8,128)(2,1)S(1)}, u32[]{:S(2)}, u32[]{:S(2)}) collective-permute-start(bf16[1024,256]{1,0:T(8,128)(2,1)S(1)} %get-tuple-element.26), channel_id=1, source_target_pairs={{4,0},{8,4},{12,8},{16,12},{20,16},{24,20},{28,24},{32,28},{36,32}... | collective-permute-start | bytes 1572872 | tf_op jit(solution)/shard_map/ppermute | solution.py:19
  99.6 7.5 copy-start.2
  99.6 8.0 %copy-start.5 = (f32[32,256,128,1]{1,2,3,0:T(8,128)S(1)}, f32[32,256,128,1]{1,2,3,0:T(8,128)}, u32[]{:S(2)}) copy-start(f32[32,256,128,1]{1,2,3,0:T(8,128)} %copy-done.4) | copy-start | bytes 12582916
  107.6 2.6 copy-start.8
  110.3 8.0 %collective-permute-start.6 = (bf16[1024,256]{1,0:T(8,128)(2,1)S(1)}, bf16[1024,256]{1,0:T(8,128)(2,1)S(1)}, u32[]{:S(2)}, u32[]{:S(2)}) collective-permute-start(bf16[1024,256]{1,0:T(8,128)(2,1)S(1)} %get-tuple-element.23), channel_id=1, source_target_pairs={{0,4},{4,8},{8,12},{12,16},{16,20},{20,24},{24,28},{28,32},{32,36}... | collective-permute-start | bytes 1572872 | tf_op jit(solution)/shard_map/ppermute | solution.py:18
  112.2 12.2 %collective-permute-start.7 = (bf16[1024,256]{1,0:T(8,128)(2,1)S(1)}, bf16[1024,256]{1,0:T(8,128)(2,1)S(1)}, u32[]{:S(2)}, u32[]{:S(2)}) collective-permute-start(bf16[1024,256]{1,0:T(8,128)(2,1)S(1)} %get-tuple-element.24), channel_id=1, source_target_pairs={{4,0},{8,4},{12,8},{16,12},{20,16},{24,20},{28,24},{32,28},{36,32}... | collective-permute-start | bytes 1572872 | tf_op jit(solution)/shard_map/ppermute | solution.py:19
  135.7 7.5 copy-start.3
  135.7 8.0 %copy-start.6 = (f32[32,256,128,1]{1,2,3,0:T(8,128)S(1)}, f32[32,256,128,1]{1,2,3,0:T(8,128)}, u32[]{:S(2)}) copy-start(f32[32,256,128,1]{1,2,3,0:T(8,128)} %copy-done.4) | copy-start | bytes 12582916
  135.7 9.2 %copy-start.9 = (f32[32,256,128,1]{1,2,3,0:T(8,128)S(1)}, f32[32,256,128,1]{1,2,3,0:T(8,128)}, u32[]{:S(2)}) copy-start(f32[32,256,128,1]{1,2,3,0:T(8,128)} %copy-done.8) | copy-start | bytes 12582916
  149.3 209.5 %all-reduce.3.cloned.1.call-start = ((), (), s32[]{:S(2)}) async-start(), calls=%async_computation.1 | async-start | bytes 2097152 | tf_op jit(solution)/shard_map/psum | solution.py:66
  252.5 156.1 %all-gather.5.cloned.1.call-start = ((), (), s32[]{:S(2)}) async-start(), calls=%async_computation.2 | async-start | bytes 5242880 | tf_op jit(solution)/shard_map/all_gather | solution.py:67
  423.6 1.9 copy-start.11
  736.3 3.2 copy-start.10
  747.7 11.2 %slice-start = ((s8[8388608]{0:T(1024)(128)(4,1)}), s8[4194304]{0:T(1024)(128)(4,1)S(1)}, s32[]{:S(2)}) async-start(s8[8388608]{0:T(1024)(128)(4,1)} %bitcast.197), calls=%async_computation.3 | async-start | bytes 8388608
  751.2 7.7 slice-start.1
Sparse Core Ops, SparseCore 0:
  149.5 94.5 all-gather.2
  252.6 106.2 all-reduce.2
  360.6 47.9 all-gather.4
where the time goes:
time: 782 us; the launch traced here: 773 us
  other arithmetic  287 us (37%)
  waiting for transfers between devices  280 us (36%)
  matrix products  91 us (12%)
  local copies, waits for them, and re-layouts  75.8 us (10%)
  starting transfers between devices  20.1 us (3%)
  between operations  18.8 us (2%)
    another operation x30, other arithmetic, shards(): lower = jnp.linalg.cholesky(gram_matrix)  172 us
    psum x1, waiting for transfers between devices, shards(): summed = lax.psum(panel, 'rows')  106 us
    all_gather x1, waiting for transfers between devices, shards(): whole_block = lax.all_gather(final, 'vecs', axis=1, tiled=True)  94.6 us
    another operation x3, other arithmetic, shards(): lax.linalg.triangular_solve(lower, identity, left_side=True, lower=True)  83.9 us
    all_gather x1, waiting for transfers between devices, shards(): lax.all_gather(summed, 'vecs', axis=0, tiled=True) / total_rows  46.9 us
    gather x4, local copies, waits for them, and re-layouts, product(): picked = stacked[local_index]  36.1 us
    dot_general x4, matrix products, product(): jnp.einsum('rjab,rjbk->rak', blocks, picked, preferred_element_type=jnp.f...  30.1 us
    another operation x24, local copies, waits for them, and re-layouts  23.8 us
  transfers between devices with their start and end apart: 11, of which 11 were waited for; matrix products, arithmetic and copies ran while one was open for 0% of the time, Pallas kernels for 0%

commit v1 on v0

--- a/solution.py
+++ b/solution.py
@@ -63,7 +63,9 @@
     identity = jnp.eye(full_width, dtype=jnp.float32)
     whole_block = lax.all_gather(final, "vecs", axis=1, tiled=True)
     panel = jnp.dot(final.T, whole_block, preferred_element_type=jnp.float32)
-    summed = lax.psum(panel, "rows")
+    summed = panel
+    for hop in (1, 2, 4, 8, 16):
+        summed = summed + lax.ppermute(summed, "rows", [(dev, dev ^ hop) for dev in range(32)])
     gram_matrix = lax.all_gather(summed, "vecs", axis=0, tiled=True) / total_rows
     lower = jnp.linalg.cholesky(gram_matrix)
     inverse = lax.linalg.triangular_solve(lower, identity, left_side=True, lower=True)

time: 782 us -> 777 us (level)
  waiting for transfers between devices: 280 us -> 265 us
  starting transfers between devices: 20.1 us -> 30.5 us
    psum x1 -> x0, waiting for transfers between devices: 106 us -> none  [shards(): summed = lax.psum(panel, 'rows')]
    ppermute x0 -> x5, waiting for transfers between devices: none -> 90.4 us  [shards(): lax.ppermute(summed, 'rows', [(dev, dev ^ hop) for dev in range(32)])]
    ppermute x0 -> x5, starting transfers between devices: none -> 10.1 us  [shards(): lax.ppermute(summed, 'rows', [(dev, dev ^ hop) for dev in range(32)])]
  transfers between devices with their start and end apart: 11 -> 15, of which waited for: 11 -> 15; matrix products, arithmetic and copies ran while one was open for 0% -> 0% of each run, Pallas kernels for 0% -> 0%
where the time goes in v1:
time: 777 us; the launch traced here: 768 us
  other arithmetic  288 us (37%)
  waiting for transfers between devices  265 us (34%)
  matrix products  90.2 us (12%)
  local copies, waits for them, and re-layouts  75 us (10%)
  starting transfers between devices  30.5 us (4%)
  between operations  19.3 us (2%)
    another operation x30, other arithmetic, shards(): lower = jnp.linalg.cholesky(gram_matrix)  173 us
    all_gather x1, waiting for transfers between devices, shards(): whole_block = lax.all_gather(final, 'vecs', axis=1, tiled=True)  94.1 us
    ppermute x5, waiting for transfers between devices, shards(): lax.ppermute(summed, 'rows', [(dev, dev ^ hop) for dev in range(32)])  90.4 us
    another operation x3, other arithmetic, shards(): lax.linalg.triangular_solve(lower, identity, left_side=True, lower=True)  83.9 us
    all_gather x1, waiting for transfers between devices, shards(): lax.all_gather(summed, 'vecs', axis=0, tiled=True) / total_rows  48 us
    gather x4, local copies, waits for them, and re-layouts, product(): picked = stacked[local_index]  36.1 us
    dot_general x4, matrix products, product(): jnp.einsum('rjab,rjbk->rak', blocks, picked, preferred_element_type=jnp.f...  30.1 us
    another operation x14, matrix products, shards(): lower = jnp.linalg.cholesky(gram_matrix)  23.1 us
  transfers between devices with their start and end apart: 15, of which 15 were waited for; matrix products, arithmetic and copies ran while one was open for 0% of the time, Pallas kernels for 0%

profile of v1, /device:TPU:1, one launch (start us, length us, event | category | flops | bytes accessed | tf_op | source)
XLA Modules:
  0.0 768.5 jit_solution(15062721935047281479)
XLA Ops:
  25.1 7.6 gather_fusion
  32.7 7.5 fusion.105
  56.7 9.5 %gather_fusion.1 = bf16[160,128,256]{2,1,0:T(8,128)(2,1)} fusion(bf16[48,128,256]{2,1,0:T(8,128)(2,1)} %bitcast.194, s32[1024]{0:T(1024)S(1)} %pad_clamp_fusion), kind=kCustom, calls=%fused_computation.1 | custom fusion | bytes 20972160 | tf_op jit(solution)/shard_map/gather | solution.py:31
  66.2 7.5 fusion.106
  90.1 9.5 %gather_fusion.2 = bf16[160,128,256]{2,1,0:T(8,128)(2,1)} fusion(bf16[48,128,256]{2,1,0:T(8,128)(2,1)} %bitcast.195, s32[1024]{0:T(1024)S(1)} %pad_clamp_fusion), kind=kCustom, calls=%fused_computation.2 | custom fusion | bytes 20972160 | tf_op jit(solution)/shard_map/gather | solution.py:31
  99.6 7.5 fusion.107
  126.3 9.5 %gather_fusion.3 = bf16[160,128,256]{2,1,0:T(8,128)(2,1)} fusion(bf16[48,128,256]{2,1,0:T(8,128)(2,1)} %bitcast.193, s32[1024]{0:T(1024)S(1)} %pad_clamp_fusion), kind=kCustom, calls=%fused_computation.3 | custom fusion | bytes 20972160 | tf_op jit(solution)/shard_map/gather | solution.py:31
  135.8 7.5 fusion.108
  150.0 94.1 %all-gather.3.cloned.1.call-done = bf16[4096,1024]{1,0:T(8,128)(2,1)} async-done(((bf16[4096,256]{1,0:T(8,128)(2,1)}), bf16[4096,1024]{1,0:T(8,128)(2,1)}) %all-gather.3.cloned.1.call-update) | async-done | bytes 8388624 | tf_op jit(solution)/shard_map/all_gather | solution.py:64
  244.1 7.4 fusion.104
  256.8 23.2 %collective-permute-done.9 = f32[256,1024]{0,1:T(8,128)S(1)} collective-permute-done((f32[256,1024]{0,1:T(8,128)S(1)}, f32[256,1024]{0,1:T(8,128)S(1)}, u32[]{:S(2)}, u32[]{:S(2)}) %collective-permute-start.9) | collective-permute-done | bytes 1048608 | tf_op jit(solution)/shard_map/ppermute | solution.py:68
  283.0 22.2 %collective-permute-done.10 = f32[256,1024]{0,1:T(8,128)S(1)} collective-permute-done((f32[256,1024]{0,1:T(8,128)S(1)}, f32[256,1024]{0,1:T(8,128)S(1)}, u32[]{:S(2)}, u32[]{:S(2)}) %collective-permute-start.10) | collective-permute-done | bytes 1048608 | tf_op jit(solution)/shard_map/ppermute | solution.py:68
  306.7 21.3 %collective-permute-done.11 = f32[256,1024]{0,1:T(8,128)S(1)} collective-permute-done((f32[256,1024]{0,1:T(8,128)S(1)}, f32[256,1024]{0,1:T(8,128)S(1)}, u32[]{:S(2)}, u32[]{:S(2)}) %collective-permute-start.11) | collective-permute-done | bytes 1048608 | tf_op jit(solution)/shard_map/ppermute | solution.py:68
  331.0 21.4 %collective-permute-done.12 = f32[256,1024]{0,1:T(8,128)S(1)} collective-permute-done((f32[256,1024]{0,1:T(8,128)S(1)}, f32[256,1024]{0,1:T(8,128)S(1)}, u32[]{:S(2)}, u32[]{:S(2)}) %collective-permute-start.12) | collective-permute-done | bytes 1048608 | tf_op jit(solution)/shard_map/ppermute | solution.py:68
  356.4 48.0 %all-gather.5.cloned.1.call-done = f32[1024,1024]{0,1:T(8,128)} async-done(((f32[256,1024]{0,1:T(8,128)}), f32[1024,1024]{0,1:T(8,128)}) %all-gather.5.cloned.1.call-update) | async-done | bytes 4194320 | tf_op jit(solution)/shard_map/all_gather | solution.py:69
  421.5 11.7 %cholesky.223 = f32[128,128]{1,0:T(8,128)S(1)} custom-call(f32[128,128]{1,0:T(8,128)S(1)} %cholesky.580), custom_call_target="Cholesky" | custom-call | tf_op jit(solution)/shard_map/jit(cholesky)/cholesky | solution.py:70
  433.2 9.8 %custom-call.62 = f32[1,128,128]{1,2,0:T(8,128)S(1)} custom-call(f32[1,128,128]{2,1,0:T(8,128)S(1)} %get-tuple-element.77), custom_call_target="InvertDiagBlocksLowerTriangular" | custom-call | tf_op jit(solution)/shard_map/jit(cholesky)/cholesky | solution.py:70
  449.4 11.9 %cholesky.244 = f32[128,128]{1,0:T(8,128)S(1)} custom-call(f32[128,128]{1,0:T(8,128)S(1)} %cholesky.584), custom_call_target="Cholesky" | custom-call | tf_op jit(solution)/shard_map/jit(cholesky)/cholesky | solution.py:70
  462.0 9.8 %custom-call.63 = f32[1,128,128]{1,2,0:T(8,128)S(1)} custom-call(f32[1,128,128]{2,1,0:T(8,128)S(1)} %get-tuple-element.74), custom_call_target="InvertDiagBlocksLowerTriangular" | custom-call | tf_op jit(solution)/shard_map/jit(cholesky)/cholesky | solution.py:70
  475.2 11.7 %cholesky.468 = f32[128,128]{1,0:T(8,128)S(1)} custom-call(f32[128,128]{1,0:T(8,128)S(1)} %cholesky.589), custom_call_target="Cholesky" | custom-call | tf_op jit(solution)/shard_map/jit(cholesky)/cholesky | solution.py:70
  488.2 9.8 %custom-call.64 = f32[1,128,128]{1,2,0:T(8,128)S(1)} custom-call(f32[1,128,128]{2,1,0:T(8,128)S(1)} %get-tuple-element.71), custom_call_target="InvertDiagBlocksLowerTriangular" | custom-call | tf_op jit(solution)/shard_map/jit(cholesky)/cholesky | solution.py:70
  501.5 12.1 %cholesky.487 = f32[128,128]{1,0:T(8,128)S(1)} custom-call(f32[128,128]{1,0:T(8,128)S(1)} %cholesky.594), custom_call_target="Cholesky" | custom-call | tf_op jit(solution)/shard_map/jit(cholesky)/cholesky | solution.py:70
  515.0 9.8 %custom-call.65 = f32[1,128,128]{1,2,0:T(8,128)S(1)} custom-call(f32[1,128,128]{2,1,0:T(8,128)S(1)} %get-tuple-element.68), custom_call_target="InvertDiagBlocksLowerTriangular" | custom-call | tf_op jit(solution)/shard_map/jit(cholesky)/cholesky | solution.py:70
  528.3 11.7 %cholesky.506 = f32[128,128]{1,0:T(8,128)S(1)} custom-call(f32[128,128]{1,0:T(8,128)S(1)} %cholesky.599), custom_call_target="Cholesky" | custom-call | tf_op jit(solution)/shard_map/jit(cholesky)/cholesky | solution.py:70
  541.3 10.0 %custom-call.66 = f32[1,128,128]{1,2,0:T(8,128)S(1)} custom-call(f32[1,128,128]{2,1,0:T(8,128)S(1)} %get-tuple-element.65), custom_call_target="InvertDiagBlocksLowerTriangular" | custom-call | tf_op jit(solution)/shard_map/jit(cholesky)/cholesky | solution.py:70
  554.6 11.7 %cholesky.526 = f32[128,128]{1,0:T(8,128)S(1)} custom-call(f32[128,128]{1,0:T(8,128)S(1)} %cholesky.604), custom_call_target="Cholesky" | custom-call | tf_op jit(solution)/shard_map/jit(cholesky)/cholesky | solution.py:70
  567.6 9.8 %custom-call.67 = f32[1,128,128]{1,2,0:T(8,128)S(1)} custom-call(f32[1,128,128]{2,1,0:T(8,128)S(1)} %get-tuple-element.62), custom_call_target="InvertDiagBlocksLowerTriangular" | custom-call | tf_op jit(solution)/shard_map/jit(cholesky)/cholesky | solution.py:70
  580.4 11.9 %cholesky.546 = f32[128,128]{1,0:T(8,128)S(1)} custom-call(f32[128,128]{1,0:T(8,128)S(1)} %cholesky.609), custom_call_target="Cholesky" | custom-call | tf_op jit(solution)/shard_map/jit(cholesky)/cholesky | solution.py:70
  593.6 9.8 %custom-call.68 = f32[1,128,128]{1,2,0:T(8,128)S(1)} custom-call(f32[1,128,128]{2,1,0:T(8,128)S(1)} %get-tuple-element.59), custom_call_target="InvertDiagBlocksLowerTriangular" | custom-call | tf_op jit(solution)/shard_map/jit(cholesky)/cholesky | solution.py:70
  606.0 11.7 %cholesky.564 = f32[128,128]{1,0:T(8,128)S(1)} custom-call(f32[128,128]{1,0:T(8,128)S(1)} %slice_subtract_fusion.6), custom_call_target="Cholesky" | custom-call | tf_op jit(solution)/shard_map/jit(cholesky)/cholesky | solution.py:70
  629.7 23.0 %while.1 = (s32[]{:T(128)}, f32[1024,1024]{1,0:T(8,128)}, s32[8,2]{0,1:T(2,128)S(1)}, f32[8,128,128]{2,1,0:T(8,128)S(1)}, s32[]{:T(128)}) while((s32[]{:T(128)}, f32[1024,1024]{1,0:T(8,128)}, s32[8,2]{0,1:T(2,128)S(1)}, f32[8,128,128]{2,1,0:T(8,128)S(1)}, s32[]{:T(128)}) %tuple.61), condition=%wide.while_cond, body=%wide.while_body.sunk | while | flops 2 | bytes 131189 | solution.py:71
  652.7 79.0 %custom-call.69 = f32[8,128,128]{1,2,0:T(8,128)S(1)} custom-call(f32[8,128,128]{2,1,0:T(8,128)S(1)} %get-tuple-element.12), custom_call_target="InvertDiagBlocksLowerTriangular" | custom-call | tf_op jit(solution)/shard_map/triangular_solve | solution.py:71
  (165 shorter events, 203.0 us)
Async XLA Ops:
  6.5 237.5 %all-gather.3.cloned.1.call-start = ((), (), s32[]{:S(2)}) async-start(), calls=%async_computation | async-start | bytes 10485760 | tf_op jit(solution)/shard_map/all_gather | solution.py:64
  7.8 10.7 %collective-permute-start = (bf16[1024,256]{1,0:T(8,128)(2,1)S(1)}, bf16[1024,256]{1,0:T(8,128)(2,1)S(1)}, u32[]{:S(2)}, u32[]{:S(2)}) collective-permute-start(bf16[1024,256]{1,0:T(8,128)(2,1)S(1)} %get-tuple-element.29), channel_id=1, source_target_pairs={{0,4},{4,8},{8,12},{12,16},{16,20},{20,24},{24,28},{28,32},{32,36}... | collective-permute-start | bytes 1572872 | tf_op jit(solution)/shard_map/ppermute | solution.py:18
  12.4 10.6 %collective-permute-start.1 = (bf16[1024,256]{1,0:T(8,128)(2,1)S(1)}, bf16[1024,256]{1,0:T(8,128)(2,1)}, u32[]{:S(2)}, u32[]{:S(2)}) collective-permute-start(bf16[1024,256]{1,0:T(8,128)(2,1)S(1)} %get-tuple-element.30), channel_id=1, source_target_pairs={{4,0},{8,4},{12,8},{16,12},{20,16},{24,20},{28,24},{32,28},{36,32}... | collective-permute-start | bytes 1572872 | tf_op jit(solution)/shard_map/ppermute | solution.py:19
  18.5 0.8 copy-start.12
  32.7 7.5 copy-start.7
  40.3 2.0 copy-start
  42.4 8.0 %collective-permute-start.2 = (bf16[1024,256]{1,0:T(8,128)(2,1)S(1)}, bf16[1024,256]{1,0:T(8,128)(2,1)S(1)}, u32[]{:S(2)}, u32[]{:S(2)}) collective-permute-start(bf16[1024,256]{1,0:T(8,128)(2,1)S(1)} %get-tuple-element.27), channel_id=1, source_target_pairs={{0,4},{4,8},{8,12},{12,16},{16,20},{20,24},{24,28},{28,32},{32,36}... | collective-permute-start | bytes 1572872 | tf_op jit(solution)/shard_map/ppermute | solution.py:18
  44.3 10.5 %collective-permute-start.3 = (bf16[1024,256]{1,0:T(8,128)(2,1)S(1)}, bf16[1024,256]{1,0:T(8,128)(2,1)S(1)}, u32[]{:S(2)}, u32[]{:S(2)}) collective-permute-start(bf16[1024,256]{1,0:T(8,128)(2,1)S(1)} %get-tuple-element.28), channel_id=1, source_target_pairs={{4,0},{8,4},{12,8},{16,12},{20,16},{24,20},{28,24},{32,28},{36,32}... | collective-permute-start | bytes 1572872 | tf_op jit(solution)/shard_map/ppermute | solution.py:19
  66.2 7.5 copy-start.1
  73.8 2.1 copy-start.4
  75.9 8.0 %collective-permute-start.4 = (bf16[1024,256]{1,0:T(8,128)(2,1)S(1)}, bf16[1024,256]{1,0:T(8,128)(2,1)S(1)}, u32[]{:S(2)}, u32[]{:S(2)}) collective-permute-start(bf16[1024,256]{1,0:T(8,128)(2,1)S(1)} %get-tuple-element.25), channel_id=1, source_target_pairs={{0,4},{4,8},{8,12},{12,16},{16,20},{20,24},{24,28},{28,32},{32,36}... | collective-permute-start | bytes 1572872 | tf_op jit(solution)/shard_map/ppermute | solution.py:18
  77.8 10.5 %collective-permute-start.5 = (bf16[1024,256]{1,0:T(8,128)(2,1)S(1)}, bf16[1024,256]{1,0:T(8,128)(2,1)S(1)}, u32[]{:S(2)}, u32[]{:S(2)}) collective-permute-start(bf16[1024,256]{1,0:T(8,128)(2,1)S(1)} %get-tuple-element.26), channel_id=1, source_target_pairs={{4,0},{8,4},{12,8},{16,12},{20,16},{24,20},{28,24},{32,28},{36,32}... | collective-permute-start | bytes 1572872 | tf_op jit(solution)/shard_map/ppermute | solution.py:19
  99.6 7.5 copy-start.2
  99.6 8.0 %copy-start.5 = (f32[32,256,128,1]{1,2,3,0:T(8,128)S(1)}, f32[32,256,128,1]{1,2,3,0:T(8,128)}, u32[]{:S(2)}) copy-start(f32[32,256,128,1]{1,2,3,0:T(8,128)} %copy-done.4) | copy-start | bytes 12582916
  107.6 2.6 copy-start.8
  110.3 8.0 %collective-permute-start.6 = (bf16[1024,256]{1,0:T(8,128)(2,1)S(1)}, bf16[1024,256]{1,0:T(8,128)(2,1)S(1)}, u32[]{:S(2)}, u32[]{:S(2)}) collective-permute-start(bf16[1024,256]{1,0:T(8,128)(2,1)S(1)} %get-tuple-element.23), channel_id=1, source_target_pairs={{0,4},{4,8},{8,12},{12,16},{16,20},{20,24},{24,28},{28,32},{32,36}... | collective-permute-start | bytes 1572872 | tf_op jit(solution)/shard_map/ppermute | solution.py:18
  112.2 12.2 %collective-permute-start.7 = (bf16[1024,256]{1,0:T(8,128)(2,1)S(1)}, bf16[1024,256]{1,0:T(8,128)(2,1)S(1)}, u32[]{:S(2)}, u32[]{:S(2)}) collective-permute-start(bf16[1024,256]{1,0:T(8,128)(2,1)S(1)} %get-tuple-element.24), channel_id=1, source_target_pairs={{4,0},{8,4},{12,8},{16,12},{20,16},{24,20},{28,24},{32,28},{36,32}... | collective-permute-start | bytes 1572872 | tf_op jit(solution)/shard_map/ppermute | solution.py:19
  135.8 7.5 copy-start.3
  135.8 8.0 %copy-start.6 = (f32[32,256,128,1]{1,2,3,0:T(8,128)S(1)}, f32[32,256,128,1]{1,2,3,0:T(8,128)}, u32[]{:S(2)}) copy-start(f32[32,256,128,1]{1,2,3,0:T(8,128)} %copy-done.4) | copy-start | bytes 12582916
  135.8 9.2 %copy-start.9 = (f32[32,256,128,1]{1,2,3,0:T(8,128)S(1)}, f32[32,256,128,1]{1,2,3,0:T(8,128)}, u32[]{:S(2)}) copy-start(f32[32,256,128,1]{1,2,3,0:T(8,128)} %copy-done.8) | copy-start | bytes 12582916
  149.4 255.0 %all-gather.5.cloned.1.call-start = ((), (), s32[]{:S(2)}) async-start(), calls=%async_computation.1 | async-start | bytes 5242880 | tf_op jit(solution)/shard_map/all_gather | solution.py:69
  251.5 4.0 collective-permute-start.8
  255.5 24.5 %collective-permute-start.9 = (f32[256,1024]{0,1:T(8,128)S(1)}, f32[256,1024]{0,1:T(8,128)S(1)}, u32[]{:S(2)}, u32[]{:S(2)}) collective-permute-start(f32[256,1024]{0,1:T(8,128)S(1)} %add.117), channel_id=1, source_target_pairs={{0,8},{4,12},{8,0},{12,4},{16,24},{20,28},{24,16},{28,20},{32,40},... | collective-permute-start | bytes 3145736 | tf_op jit(solution)/shard_map/ppermute | solution.py:68
  280.1 25.0 %collective-permute-start.10 = (f32[256,1024]{0,1:T(8,128)S(1)}, f32[256,1024]{0,1:T(8,128)S(1)}, u32[]{:S(2)}, u32[]{:S(2)}) collective-permute-start(f32[256,1024]{0,1:T(8,128)S(1)} %add.118), channel_id=1, source_target_pairs={{0,16},{4,20},{8,24},{12,28},{16,0},{20,4},{24,8},{28,12},{32,48},... | collective-permute-start | bytes 3145736 | tf_op jit(solution)/shard_map/ppermute | solution.py:68
  305.3 22.6 %collective-permute-start.11 = (f32[256,1024]{0,1:T(8,128)S(1)}, f32[256,1024]{0,1:T(8,128)S(1)}, u32[]{:S(2)}, u32[]{:S(2)}) collective-permute-start(f32[256,1024]{0,1:T(8,128)S(1)} %add.119), channel_id=1, source_target_pairs={{0,32},{4,36},{8,40},{12,44},{16,48},{20,52},{24,56},{28,60},{32,0... | collective-permute-start | bytes 3145736 | tf_op jit(solution)/shard_map/ppermute | solution.py:68
  328.1 24.4 %collective-permute-start.12 = (f32[256,1024]{0,1:T(8,128)S(1)}, f32[256,1024]{0,1:T(8,128)S(1)}, u32[]{:S(2)}, u32[]{:S(2)}) collective-permute-start(f32[256,1024]{0,1:T(8,128)S(1)} %add.120), channel_id=1, source_target_pairs={{0,64},{4,68},{8,72},{12,76},{16,80},{20,84},{24,88},{28,92},{32,9... | collective-permute-start | bytes 3145736 | tf_op jit(solution)/shard_map/ppermute | solution.py:68
  419.4 2.0 copy-start.11
  731.8 3.2 copy-start.10
  743.1 11.2 %slice-start = ((s8[8388608]{0:T(1024)(128)(4,1)}), s8[4194304]{0:T(1024)(128)(4,1)S(1)}, s32[]{:S(2)}) async-start(s8[8388608]{0:T(1024)(128)(4,1)} %bitcast.197), calls=%async_computation.2 | async-start | bytes 8388608
  746.6 7.7 %slice-start.1 = ((s8[8388608]{0:T(1024)(128)(4,1)}), s8[4194304]{0:T(1024)(128)(4,1)S(1)}, s32[]{:S(2)}) async-start(s8[8388608]{0:T(1024)(128)(4,1)} %bitcast.197), calls=%async_computation.3 | async-start | bytes 8388608
Sparse Core Ops, SparseCore 0:
  149.5 94.5 all-gather.2
  353.7 50.6 all-gather.4
